TPU v7x, 32 devices: a whole 2x2x4 slice. The times are simulated.
32 devices in a mesh: groups: 2 (over y), tile: 8 (over z, x), feat: 2 (over core).
Axes of the slice: x: 2, y: 2, z: 4, core: 2. Of those that a mesh axis runs over, the one named last changes fastest.
Arguments:
- preacts: bfloat16 [3, 16384, 256], P(None, ('tile', 'feat'), 'groups'), parts along dimension 2, may hold values from -6 to 6
- targets: bfloat16 [3, 512, 1152], P(None, ('groups', 'tile', 'feat')), parts along dimension 1, may hold values from -4 to 4
- decoder: bfloat16 [16, 2, 12288, 2304], P(('groups', 'tile'), 'feat'), parts along dimension 0, may hold values from -0.02734375 to 0.02734375
- owner_list: int32 [16384, 6, 1], P(('tile', 'feat')), may hold values from 0 to 7; in each aligned block of 6144 rows (0 to 6143, 6144 to 12287, ..., all dimensions but the last counted through in order) at most 1536 rows name the same one
- tile_source: int32 [6], replicated, may hold values from 0 to 2, as said below
- tile_target: int32 [6], replicated, may hold values from 0 to 2, as said below
- row_order: int32 [4, 64], P('groups'), parts along dimension 0, may hold values from 0 to 63, each once within a row
Outputs:
- residual: float32 [3, 512, 1152], P(None, ('groups', 'tile', 'feat')), parts along dimension 1
- feature_grad: float32 [3, 16384, 256], P(None, ('tile', 'feat'), 'groups'), parts along dimension 2
There are 2 independent parts, one for each index of `groups`. A program takes and returns all parts, laid end to end along the dimension named above; an argument that names none is the same for every part. Nothing has to cross between parts.
Inputs may be any that keep to these rules, and one draw needn't show every extreme that they name: `owner_list`: among the 6144 rows of one device (features f with f // 1024 equal, all tiles), no owner is named more than 1536 times, and in some device one owner exactly 1536 times; every owner is named somewhere. `tile_source`: together with tile_target, every pair of layers s <= t appears exactly once. tile_target[k] >= tile_source[k]. `row_order`: each row is a permutation.
All inputs are finite; a program needn't handle non-finite values.
Results may differ from a plain program's by a relative error of at most 0.0027.
Values may be sent and summed in bfloat16 or wider, within the bound.
A program may use at most 128 MiB of HBM per device.

v0:
```python
import jax
import jax.numpy as jnp
from jax import lax
from jax.sharding import PartitionSpec as P


def reorder(values, indices):
    leading = values.shape[:-1]
    blocks, block_span = indices.shape
    shaped = values.reshape(leading + (blocks, block_span))
    block_col = jnp.arange(blocks, dtype=jnp.int32)[:, None]
    return shaped[..., block_col, indices].reshape(values.shape)


def inverse_order(row_order):
    positions = lax.broadcasted_iota(jnp.int32, row_order.shape, 1)
    block_ids = lax.broadcasted_iota(jnp.int32, row_order.shape, 0)
    inverse = jnp.zeros(row_order.shape, jnp.int32)
    return inverse.at[block_ids, row_order].set(positions)


def on_device(preacts, targets, decoder, owner_list, tile_source, tile_target, row_order):
    owners = lax.axis_size("tile")
    layers, feat_dev, tokens = preacts.shape
    tile_count = tile_source.shape[0]
    slot_count = decoder.shape[2]
    capacity = slot_count // owners
    model_width = decoder.shape[3]
    inverse = inverse_order(row_order)
    active = jax.nn.relu(preacts.astype(jnp.float32)).astype(jnp.bfloat16)
    natural = reorder(active, inverse)
    picked = natural[tile_source]
    row_values = jnp.transpose(picked, (1, 0, 2)).reshape(feat_dev * tile_count, tokens)
    destination = owner_list.reshape(-1)
    count_rows = destination.shape[0]
    same_owner = destination[:, None] == destination[None, :]
    before = lax.broadcasted_iota(jnp.int32, (count_rows, count_rows), 0) < lax.broadcasted_iota(
        jnp.int32, (count_rows, count_rows), 1
    )
    slot_rank = jnp.sum((same_owner & before).astype(jnp.int32), axis=0)
    slot_of = destination * capacity + slot_rank
    slot_match = lax.broadcasted_iota(jnp.int32, (slot_count, count_rows), 0) == slot_of[None, :]
    packed = jnp.dot(
        slot_match.astype(jnp.bfloat16), row_values, preferred_element_type=jnp.float32
    ).astype(jnp.bfloat16)
    tile_of_row = lax.broadcasted_iota(jnp.int32, (feat_dev, tile_count), 1).reshape(-1)
    tile_slot = jnp.sum(jnp.where(slot_match, tile_of_row[None, :] + 1, 0), axis=1) - 1
    received, tile_recv = (
        lax.all_to_all(
            packed.reshape(owners, capacity, tokens),
            "tile",
            split_axis=0,
            concat_axis=0,
            tiled=True,
        ),
        lax.all_to_all(
            tile_slot.reshape(owners, capacity), "tile", split_axis=0, concat_axis=0, tiled=True
        ),
    )
    received = received.reshape(slot_count, tokens)
    tile_recv = tile_recv.reshape(slot_count)
    tile_ids = lax.broadcasted_iota(jnp.int32, (slot_count, tile_count), 1)
    target_slot = jnp.sum(
        jnp.where(tile_recv[:, None] == tile_ids, tile_target[None, :], 0), axis=1
    )
    occupied = tile_recv >= 0
    weights = decoder[0, 0]
    pieces = []
    for target_layer in range(layers):
        chosen = (occupied & (target_slot == target_layer))[:, None]
        masked = jnp.where(chosen, received, jnp.zeros_like(received))
        pieces.append(
            lax.dot_general(
                masked, weights, (((0,), (0,)), ((), ())), preferred_element_type=jnp.float32
            )
        )
    partial_value = jnp.stack(pieces).reshape(layers, 2 * tokens, model_width // 2)
    own_sums = lax.psum_scatter(partial_value, ("tile", "feat"), scatter_dimension=1, tiled=True)
    residual = own_sums - targets.astype(jnp.float32)
    spread = lax.all_gather(
        residual.astype(jnp.bfloat16), ("tile", "feat"), axis=1, tiled=True
    ).reshape(layers, tokens, model_width)
    slot_grad = jnp.zeros((slot_count, tokens), jnp.float32)
    for target_layer in range(layers):
        chosen = (occupied & (target_slot == target_layer))[:, None]
        product = lax.dot_general(
            weights,
            spread[target_layer],
            (((1,), (1,)), ((), ())),
            preferred_element_type=jnp.float32,
        )
        slot_grad = slot_grad + jnp.where(chosen, product, 0.0)
    returned = lax.all_to_all(
        slot_grad.reshape(owners, capacity, tokens), "tile", split_axis=0, concat_axis=0, tiled=True
    ).reshape(slot_count, tokens)
    row_grad = returned[slot_of].reshape(feat_dev, tile_count, tokens)
    layer_grad = jnp.stack(
        [
            jnp.sum(jnp.where((tile_source == source_layer)[None, :, None], row_grad, 0.0), axis=1)
            for source_layer in range(layers)
        ]
    )
    natural_pre = reorder(preacts, inverse)
    layer_grad = jnp.where(natural_pre > 0, layer_grad, 0.0)
    feature_grad = reorder(layer_grad, row_order)
    return (residual, feature_grad)


def solution(mesh):
    return jax.shard_map(
        on_device,
        mesh=mesh,
        in_specs=(
            P(None, ("tile", "feat"), "groups"),
            P(None, ("groups", "tile", "feat"), None),
            P(("groups", "tile"), "feat", None, None),
            P(("tile", "feat"), None, None),
            P(),
            P(),
            P("groups", None),
        ),
        out_specs=(P(None, ("groups", "tile", "feat"), None), P(None, ("tile", "feat"), "groups")),
        check_vma=False,
    )
```

profile of v0, /device:TPU:0, one launch (start us, length us, event | category | flops | bytes accessed | tf_op | source)
XLA Modules:
  0.0 728.6 jit_solution(1906964047460413758)
XLA Ops:
  8.6 34.1 %convert_reduce_fusion = s32[6144]{0:T(1024)S(1)} fusion(s32[6144]{0:T(1024)S(1)} %reshape.199), kind=kLoop, calls=%fused_computation.10 | loop fusion | flops 188737536 | bytes 49152 | tf_op jit(solution)/shard_map/reduce_sum | solution.py:40
  43.1 45.1 %select_reduce_fusion = s32[12288]{0:T(1024)S(1)} fusion(s32[6144]{0:T(1024)S(1)} %add.85, s32[6144]{0:T(1024)S(1)} %multiply_add_fusion), kind=kLoop, calls=%fused_computation.6 | loop fusion | flops 226480128 | bytes 98304 | tf_op jit(solution)/shard_map/reduce_sum | solution.py:47
  88.8 7.6 %all-to-all-start = ((s32[8,1,1536]{2,1,0:T(1,128)}), s32[8,1,1536]{2,1,0:T(1,128)S(1)}, u32[]{:S(2)}, u32[]{:S(2)}) async-start(s32[8,1,1536]{2,1,0:T(1,128)} %bitcast), calls=%async_computation | async-start | bytes 98304 | tf_op jit(solution)/shard_map/all_to_all | solution.py:56
  98.3 6.4 scatter_fusion
  113.1 55.0 %fusion.15 = bf16[12288,128]{1,0:T(8,128)(2,1)} fusion(bf16[6144,128]{1,0:T(8,128)(2,1)} %reshape.202, s32[6144]{0:T(1024)S(1)} %multiply_add_fusion), kind=kOutput, calls=%fused_computation.25 | convolution fusion | flops 19404423168 | bytes 4743168 | tf_op jit(solution)/shard_map/dot_general | solution.py:43
  168.1 6.1 all-to-all-start.1
  176.0 68.5 %all-to-all-done.1 = bf16[8,1536,128]{2,1,0:T(8,128)(2,1)S(1)} async-done(((bf16[8,1536,128]{2,1,0:T(8,128)(2,1)}), bf16[8,1536,128]{2,1,0:T(8,128)(2,1)S(1)}, u32[]{:S(2)}, u32[]{:S(2)}) %all-to-all-start.1) | async-done | bytes 3145760 | tf_op jit(solution)/shard_map/all_to_all | solution.py:49
  246.1 9.0 %broadcast_select_fusion.2 = (bf16[8,1536,128]{2,1,0:T(8,128)(2,1)S(1)}, bf16[8,1536,128]{2,1,0:T(8,128)(2,1)S(1)}, bf16[8,1536,128]{2,1,0:T(8,128)(2,1)}) fusion(bf16[8,1536,128]{2,1,0:T(8,128)(2,1)} %copy-done.2, pred[8,1536]{1,0:T(8,128)(4,1)S(1)} %get-tuple-element.24, pred[8,1536]{1,0:T(8,128)(4,1)S(1)} %get-tuple-element.35, ...), kind=kLoop, calls=%fused_computation.38 | loop fusion | flops 4718592 | bytes 12619776 | tf_op jit(solution)/shard_map/jit(_where)/select_n | solution.py:71
  255.1 21.1 %fusion.9 = f32[128,2304]{1,0:T(8,128)} fusion(bf16[12288,128]{1,0:T(8,128)(2,1)S(1)} %bitcast.94, bf16[1,1,12288,2304]{3,2,1,0:T(8,128)(2,1)} %param.9), kind=kOutput, calls=%fused_computation.19 | convolution fusion | flops 7247757312 | bytes 60948480 | tf_op jit(solution)/shard_map/dot_general | solution.py:73
  278.6 22.1 %fusion.11 = f32[128,2304]{1,0:T(8,128)} fusion(bf16[12288,128]{1,0:T(8,128)(2,1)} %bitcast.93, bf16[1,1,12288,2304]{3,2,1,0:T(8,128)(2,1)} %param.9), kind=kOutput, calls=%fused_computation.21 | convolution fusion | flops 7247757312 | bytes 60948480 | tf_op jit(solution)/shard_map/dot_general | solution.py:73
  303.2 21.0 %fusion.13 = f32[128,2304]{1,0:T(8,128)} fusion(bf16[12288,128]{1,0:T(8,128)(2,1)S(1)} %bitcast.92, bf16[1,1,12288,2304]{3,2,1,0:T(8,128)(2,1)} %param.9), kind=kOutput, calls=%fused_computation.23 | convolution fusion | flops 7247757312 | bytes 60948480 | tf_op jit(solution)/shard_map/dot_general | solution.py:73
  328.4 67.0 %reduce-scatter.2.cloned.1.call-done = f32[3,16,1152]{2,1,0:T(8,128)} async-done(((f32[3,256,1152]{2,1,0:T(8,128)}), f32[3,16,1152]{2,1,0:T(8,128)}) %reduce-scatter.2.cloned.1.call-update) | async-done | bytes 221200 | tf_op jit(solution)/shard_map/reduce_scatter | solution.py:78
  397.2 40.5 %all-gather.2.cloned.1.call-done = bf16[3,256,1152]{2,1,0:T(8,128)(2,1)} async-done(((bf16[3,16,1152]{2,1,0:T(8,128)(2,1)}), bf16[3,256,1152]{2,1,0:T(8,128)(2,1)}) %all-gather.2.cloned.1.call-update) | async-done | bytes 1769488 | tf_op jit(solution)/shard_map/all_gather | solution.py:80
  439.9 27.0 %fusion.28 = f32[128,12288]{1,0:T(8,128)} fusion(bf16[128,2304]{1,0:T(8,128)(2,1)S(1)} %squeeze.15, bf16[1,1,12288,2304]{3,2,1,0:T(8,128)(2,1)} %param.9, pred[12288]{0:T(1024)(128)(4,1)S(1)} %copy-done.14), kind=kOutput, calls=%fused_computation.30 | convolution fusion | flops 7249330176 | bytes 63516672 | tf_op jit(solution)/shard_map/dot_general | solution.py:86
  466.9 27.0 %fusion.25 = f32[128,12288]{1,0:T(8,128)} fusion(bf16[128,2304]{1,0:T(8,128)(2,1)S(1)} %squeeze.14, bf16[1,1,12288,2304]{3,2,1,0:T(8,128)(2,1)} %param.9, pred[12288]{0:T(1024)(128)(4,1)S(1)} %copy-done.13), kind=kOutput, calls=%fused_computation.29 | convolution fusion | flops 7249330176 | bytes 63516672 | tf_op jit(solution)/shard_map/dot_general | solution.py:86
  493.9 30.4 %fusion.22 = f32[128,12288]{1,0:T(8,128)} fusion(f32[128,12288]{1,0:T(8,128)} %fusion.28, f32[128,12288]{1,0:T(8,128)} %fusion.25, bf16[128,2304]{1,0:T(8,128)(2,1)S(1)} %squeeze.13, bf16[1,1,12288,2304]{3,2,1,0:T(8,128)(2,1)} %param.9, pred[12288]{0:T(1024)(128)(4,1)S(1)} %get-tuple-element.15), kind=kOutput, calls=%fused_computation.28 | convolution fusion | flops 7252475904 | bytes 76099584 | tf_op jit(solution)/shard_map/dot_general | solution.py:86
  524.3 6.0 copy.90
  530.4 4.9 all-to-all-start.2
  539.8 134.2 %all-to-all-done.2 = f32[8,1536,128]{1,2,0:T(8,128)} async-done(((f32[8,1536,128]{1,2,0:T(8,128)}), f32[8,1536,128]{1,2,0:T(8,128)}, u32[]{:S(2)}, u32[]{:S(2)}) %all-to-all-start.2) | async-done | bytes 6291488 | tf_op jit(solution)/shard_map/all_to_all | solution.py:93
  674.1 6.6 copy.76
  680.6 18.9 %gather_fusion.3 = f32[6144,128]{1,0:T(8,128)S(1)} fusion(f32[12288,128]{1,0:T(8,128)} %bitcast.89, s32[6144]{0:T(1024)S(1)} %broadcast_clamp_fusion), kind=kCustom, calls=%fused_computation.3 | custom fusion | bytes 6316032 | tf_op jit(solution)/shard_map/gather | solution.py:96
  701.9 6.5 select_reduce_fusion.3
  712.5 3.2 maximum_select_fusion
  715.6 3.1 gather_fusion.4
  (104 shorter events, 42.5 us)
Async XLA Ops:
  7.2 89.2 %copy-start.8 = (bf16[3,1024,128]{2,1,0:T(8,128)(2,1)S(1)}, bf16[3,1024,128]{2,1,0:T(8,128)(2,1)}, u32[]{:S(2)}) copy-start(bf16[3,1024,128]{2,1,0:T(8,128)(2,1)} %param.7) | copy-start | bytes 2359300
  42.7 46.1 %copy-start.11 = (s32[6144]{0:T(1024)}, s32[6144]{0:T(1024)S(1)}, u32[]{:S(2)}) copy-start(s32[6144]{0:T(1024)S(1)} %convert_reduce_fusion) | copy-start | bytes 73732
  43.1 54.5 %copy-start.15 = (s32[2,64]{1,0:T(2,128)S(1)}, s32[2,64]{1,0:T(2,128)}, u32[]{:S(2)}) copy-start(s32[2,64]{1,0:T(2,128)} %param.13) | copy-start | bytes 1540
  88.8 79.3 %all-to-all-start = ((s32[8,1,1536]{2,1,0:T(1,128)}), s32[8,1,1536]{2,1,0:T(1,128)S(1)}, u32[]{:S(2)}, u32[]{:S(2)}) async-start(s32[8,1,1536]{2,1,0:T(1,128)} %bitcast), calls=%async_computation | async-start | bytes 98304 | tf_op jit(solution)/shard_map/all_to_all | solution.py:56
  104.8 2.3 copy-start
  104.8 2.4 copy-start.18
  168.1 6.7 copy-start.17
  168.1 76.3 %all-to-all-start.1 = ((bf16[8,1536,128]{2,1,0:T(8,128)(2,1)}), bf16[8,1536,128]{2,1,0:T(8,128)(2,1)S(1)}, u32[]{:S(2)}, u32[]{:S(2)}) async-start(bf16[8,1536,128]{2,1,0:T(8,128)(2,1)} %bitcast.100), calls=%async_computation.1 | async-start | bytes 6291456 | tf_op jit(solution)/shard_map/all_to_all | solution.py:49
  174.3 221.2 %reduce-scatter.2.cloned.1.call-start = ((), (), s32[]{:S(2)}) async-start(), calls=%async_computation.4 | async-start | bytes 3760128 | tf_op jit(solution)/shard_map/reduce_scatter | solution.py:78
  244.4 1.7 copy-start.2
  324.2 1.6 copy-start.5
  324.2 2.0 copy-start.6
  328.2 67.3 %copy-start.9 = (bf16[3,16,1152]{2,1,0:T(8,128)(2,1)S(1)}, bf16[3,16,1152]{2,1,0:T(8,128)(2,1)}, u32[]{:S(2)}) copy-start(bf16[3,16,1152]{2,1,0:T(8,128)(2,1)} %param.8) | copy-start | bytes 331780
  328.2 109.5 %all-gather.2.cloned.1.call-start = ((), (), s32[]{:S(2)}) async-start(), calls=%async_computation.5 | async-start | bytes 1880064 | tf_op jit(solution)/shard_map/all_gather | solution.py:80
  397.2 42.7 %copy-start.14 = (pred[12288]{0:T(1024)(128)(4,1)S(1)}, pred[12288]{0:T(1024)(128)(4,1)}, u32[]{:S(2)}) copy-start(pred[12288]{0:T(1024)(128)(4,1)} %get-tuple-element.32) | copy-start | bytes 36868
  439.9 27.0 %copy-start.13 = (pred[12288]{0:T(1024)(128)(4,1)S(1)}, pred[12288]{0:T(1024)(128)(4,1)}, u32[]{:S(2)}) copy-start(pred[12288]{0:T(1024)(128)(4,1)} %get-tuple-element.18) | copy-start | bytes 36868
  530.4 4.9 copy-start.4
  530.4 5.6 copy-start.1
  530.4 143.7 %all-to-all-start.2 = ((f32[8,1536,128]{1,2,0:T(8,128)}), f32[8,1536,128]{1,2,0:T(8,128)}, u32[]{:S(2)}, u32[]{:S(2)}) async-start(f32[8,1536,128]{1,2,0:T(8,128)} %bitcast.90), calls=%async_computation.3 | async-start | bytes 12582912 | tf_op jit(solution)/shard_map/all_to_all | solution.py:93
  535.2 2.4 copy-start.10
  535.3 3.0 copy-start.16
  535.3 3.1 copy-start.19
  535.3 3.1 copy-start.12
  708.4 4.1 copy-start.7
  (1 other events, 1.5 us)
Sparse Core Ops, SparseCore 0:
  328.3 67.1 reduce-scatter.1
  398.4 39.2 all-gather.1
where the time goes:
time: 732 us; the launch traced here: 729 us
  waiting for transfers between devices  310 us (42%)
  matrix products  204 us (28%)
  other arithmetic  105 us (14%)
  local copies, waits for them, and re-layouts  75.2 us (10%)
  starting transfers between devices  19.4 us (3%)
  between operations  14.8 us (2%)
    all_to_all x1, waiting for transfers between devices, on_device(): lax.all_to_all(slot_grad.reshape(owners, capacity, tokens), 'tile', split...  134 us
    dot_general x3, matrix products, on_device(): lax.dot_general(weights, spread[target_layer], (((1,), (1,)), ((), ())),...  84.4 us
    all_to_all x1, waiting for transfers between devices, on_device(): lax.all_to_all(packed.reshape(owners, capacity, tokens), 'tile', split_ax...  68.5 us
    reduce_scatter x1, waiting for transfers between devices, on_device(): lax.psum_scatter(partial_value, ('tile', 'feat'), scatter_dimension=1, ti...  67 us
    dot_general x3, matrix products, on_device(): lax.dot_general(masked, weights, (((0,), (0,)), ((), ())), preferred_elem...  64.2 us
    dot_general x1, matrix products, on_device(): jnp.dot(slot_match.astype(jnp.bfloat16), row_values, preferred_element_ty...  55 us
    reduce_sum x1, other arithmetic, on_device(): jnp.sum(jnp.where(slot_match, tile_of_row[None, :] + 1, 0), axis=1) - 1  45.1 us
    all_gather x1, waiting for transfers between devices, on_device(): lax.all_gather(residual.astype(jnp.bfloat16), ('tile', 'feat'), axis=1, t...  40.5 us
  transfers between devices with their start and end apart: 5, of which 4 were waited for; matrix products, arithmetic and copies ran while one was open for 11% of the time, Pallas kernels for 0%

commit v1 on v0

v1 whole, which is shorter than its diff:
```python
import math

import jax
import jax.numpy as jnp
from jax import lax
from jax.sharding import PartitionSpec as P


def permutation_matrix(row_order):
    blocks, span = row_order.shape
    token = (row_order + span * jnp.arange(blocks, dtype=jnp.int32)[:, None]).reshape(-1)
    ids = lax.broadcasted_iota(jnp.int32, (blocks * span, blocks * span), 1)
    return (token[:, None] == ids).astype(jnp.bfloat16)


def ranks(destination, owners):
    rows = destination.shape[0]
    span = math.gcd(rows, 128)
    blocks = rows // span
    hot = lax.broadcasted_iota(jnp.int32, (owners, rows), 0) == destination[None, :]
    parts = hot.astype(jnp.bfloat16).reshape(owners, blocks, span)

    def earlier(n):
        return (
            lax.broadcasted_iota(jnp.int32, (n, n), 0) < lax.broadcasted_iota(jnp.int32, (n, n), 1)
        ).astype(jnp.bfloat16)

    inner = jnp.dot(parts, earlier(span), preferred_element_type=jnp.float32)
    totals = jnp.sum(parts.astype(jnp.float32), axis=2).astype(jnp.bfloat16)
    outer = jnp.dot(totals, earlier(blocks), preferred_element_type=jnp.float32)
    count = (inner + outer[:, :, None]).reshape(owners, rows)
    return jnp.sum(jnp.where(hot, count, 0.0), axis=0).astype(jnp.int32)


def on_device(preacts, targets, decoder, owner_list, tile_source, tile_target, row_order):
    owners = lax.axis_size("tile")
    layers, feat_dev, tokens = preacts.shape
    tile_count = tile_source.shape[0]
    slot_count = decoder.shape[2]
    capacity = slot_count // owners
    model_width = decoder.shape[3]
    to_token = permutation_matrix(row_order)
    active = jnp.maximum(preacts, jnp.zeros_like(preacts))
    natural = jnp.dot(active, to_token, preferred_element_type=jnp.float32).astype(jnp.bfloat16)
    picked = jnp.zeros((feat_dev, tile_count, tokens), jnp.bfloat16)
    for layer in range(layers):
        picked = jnp.where(
            (tile_source == layer)[None, :, None], natural[layer][:, None, :], picked
        )
    count_rows = feat_dev * tile_count
    row_values = picked.reshape(count_rows, tokens)
    destination = owner_list.reshape(-1)
    slot_of = destination * capacity + ranks(destination, owners)
    tile_of_row = lax.broadcasted_iota(jnp.int32, (feat_dev, tile_count, tokens), 1)
    tile_of_row = (tile_of_row + 1).astype(jnp.bfloat16).reshape(count_rows, tokens)
    slot_match = lax.broadcasted_iota(jnp.int32, (slot_count, count_rows), 0) == slot_of[None, :]
    packed = jnp.dot(
        slot_match.astype(jnp.bfloat16),
        jnp.concatenate([row_values, tile_of_row], axis=1),
        preferred_element_type=jnp.float32,
    ).astype(jnp.bfloat16)
    tile_slot = packed[:, tokens].astype(jnp.int32) - 1
    tile_recv = lax.all_to_all(
        tile_slot.reshape(owners, capacity), "tile", split_axis=0, concat_axis=0, tiled=True
    ).reshape(slot_count)
    received = lax.all_to_all(
        packed[:, :tokens].reshape(owners, capacity, tokens),
        "tile",
        split_axis=0,
        concat_axis=0,
        tiled=True,
    ).reshape(slot_count, tokens)
    tile_ids = lax.broadcasted_iota(jnp.int32, (slot_count, tile_count), 1)
    target_slot = jnp.sum(
        jnp.where(tile_recv[:, None] == tile_ids, tile_target[None, :] + 1, 0), axis=1
    ) - 1
    weights = decoder[0, 0]
    masked = jnp.concatenate(
        [
            jnp.where((target_slot == layer)[:, None], received, jnp.zeros_like(received))
            for layer in range(layers)
        ],
        axis=1,
    )
    partial_value = lax.dot_general(
        masked, weights, (((0,), (0,)), ((), ())), preferred_element_type=jnp.float32
    ).reshape(layers, 2 * tokens, model_width // 2)
    own_sums = lax.psum_scatter(partial_value, ("tile", "feat"), scatter_dimension=1, tiled=True)
    residual = own_sums - targets.astype(jnp.float32)
    spread = lax.all_gather(
        residual.astype(jnp.bfloat16), ("tile", "feat"), axis=1, tiled=True
    ).reshape(layers, tokens, model_width)
    by_column = [
        jnp.dot(to_token, spread[layer], preferred_element_type=jnp.float32).astype(jnp.bfloat16)
        for layer in range(layers)
    ]
    product = lax.dot_general(
        weights,
        jnp.concatenate(by_column, axis=0),
        (((1,), (1,)), ((), ())),
        preferred_element_type=jnp.float32,
    ).astype(jnp.bfloat16)
    slot_grad = jnp.zeros((slot_count, tokens), jnp.bfloat16)
    for layer in range(layers):
        slot_grad = jnp.where(
            (target_slot == layer)[:, None],
            product[:, layer * tokens : (layer + 1) * tokens],
            slot_grad,
        )
    returned = lax.all_to_all(
        slot_grad.reshape(owners, capacity, tokens), "tile", split_axis=0, concat_axis=0, tiled=True
    ).reshape(slot_count, tokens)
    row_grad = returned.astype(jnp.float32)[slot_of].reshape(feat_dev, tile_count, tokens)
    layer_grad = jnp.stack(
        [
            jnp.sum(jnp.where((tile_source == layer)[None, :, None], row_grad, 0.0), axis=1)
            for layer in range(layers)
        ]
    )
    return (residual, jnp.where(preacts > 0, layer_grad, 0.0))


def solution(mesh):
    return jax.shard_map(
        on_device,
        mesh=mesh,
        in_specs=(
            P(None, ("tile", "feat"), "groups"),
            P(None, ("groups", "tile", "feat"), None),
            P(("groups", "tile"), "feat", None, None),
            P(("tile", "feat"), None, None),
            P(),
            P(),
            P("groups", None),
        ),
        out_specs=(P(None, ("groups", "tile", "feat"), None), P(None, ("tile", "feat"), "groups")),
        check_vma=False,
    )
```

time: 732 us -> 485 us (0.66)
  matrix products: 204 us -> 120 us
  other arithmetic: 105 us -> 33.5 us
  waiting for transfers between devices: 310 us -> 250 us
  local copies, waits for them, and re-layouts: 75.2 us -> 51.5 us
    reduce_sum x4 -> x3, other arithmetic: 85.9 us -> 6.91 us  [the longest x1 6.58 us: on_device(): jnp.sum(jnp.where((tile_source == layer)[None, :, None], row_grad, 0.0),...]
    all_to_all x1, waiting for transfers between devices: 134 us -> 69.8 us  [on_device(): lax.all_to_all(slot_grad.reshape(owners, capacity, tokens), 'tile', split...]
    dot_general x4 -> x8, matrix products: 139 us -> 90 us  [the longest x1 55.6 us: on_device(): jnp.dot(slot_match.astype(jnp.bfloat16), jnp.concatenate([row_values, til...]
    dot_general x3 -> x1, matrix products: 64.2 us -> 29.8 us  [on_device(): lax.dot_general(masked, weights, (((0,), (0,)), ((), ())), preferred_elem...]
    another operation x6 -> x0, local copies, waits for them, and re-layouts: 10 us -> none  [the longest x3 6.57 us: on_device(): jnp.stack(pieces).reshape(layers, 2 * tokens, model_width // 2)]
    gather x6 -> x1, local copies, waits for them, and re-layouts: 27.5 us -> 18.9 us  [on_device(): returned.astype(jnp.float32)[slot_of].reshape(feat_dev, tile_count, tokens)]
    select_n x4 -> x5, other arithmetic: 12.2 us -> 20.2 us  [the longest x1 9.23 us: on_device(): jnp.where((tile_source == layer)[None, :, None], natural[layer][:, None,...]
  transfers between devices with their start and end apart: 5 -> 5, of which waited for: 4 -> 5; matrix products, arithmetic and copies ran while one was open for 11% -> 1% of each run, Pallas kernels for 0% -> 0%
where the time goes in v1:
time: 485 us; the launch traced here: 484 us
  waiting for transfers between devices  250 us (52%)
  matrix products  120 us (25%)
  local copies, waits for them, and re-layouts  51.5 us (11%)
  other arithmetic  33.5 us (7%)
  starting transfers between devices  14.9 us (3%)
  between operations  14.5 us (3%)
    all_to_all x1, waiting for transfers between devices, on_device(): lax.all_to_all(slot_grad.reshape(owners, capacity, tokens), 'tile', split...  69.8 us
    all_to_all x1, waiting for transfers between devices, on_device(): lax.all_to_all(packed[:, :tokens].reshape(owners, capacity, tokens), 'til...  69.2 us
    reduce_scatter x1, waiting for transfers between devices, on_device(): lax.psum_scatter(partial_value, ('tile', 'feat'), scatter_dimension=1, ti...  67.2 us
    dot_general x1, matrix products, on_device(): jnp.dot(slot_match.astype(jnp.bfloat16), jnp.concatenate([row_values, til...  55.6 us
    all_gather x1, waiting for transfers between devices, on_device(): lax.all_gather(residual.astype(jnp.bfloat16), ('tile', 'feat'), axis=1, t...  40.6 us
    dot_general x1, matrix products, on_device(): lax.dot_general(weights, jnp.concatenate(by_column, axis=0), (((1,), (1,)...  32.6 us
    dot_general x1, matrix products, on_device(): lax.dot_general(masked, weights, (((0,), (0,)), ((), ())), preferred_elem...  29.8 us
    gather x1, local copies, waits for them, and re-layouts, on_device(): returned.astype(jnp.float32)[slot_of].reshape(feat_dev, tile_count, tokens)  18.9 us
  transfers between devices with their start and end apart: 5, of which 5 were waited for; matrix products, arithmetic and copies ran while one was open for 1% of the time, Pallas kernels for 0%

profile of v1, /device:TPU:0, one launch (start us, length us, event | category | flops | bytes accessed | tf_op | source)
XLA Modules:
  0.0 484.5 jit_solution(4308635797513299236)
XLA Ops:
  19.7 9.2 %select_select_fusion = bf16[6144,128]{1,0:T(8,128)(2,1)S(1)} fusion(bf16[6144,128]{1,0:T(8,128)(2,1)} %broadcast_in_dim.157, bf16[6144,128]{1,0:T(8,128)(2,1)} %broadcast_in_dim.163, bf16[6144,128]{1,0:T(8,128)(2,1)} %broadcast_in_dim.169, pred[6144]{0:T(1024)(128)(4,1)S(1)} %broadcast_in_dim.165, pred[6144]{0:T(1024)(128)(4,1)S(1)} %broadcast_in_dim.159, ...), kind=kLoop, calls=%fused_computation.39 | loop fusion | flops 2359296 | bytes 6309888 | tf_op jit(solution)/shard_map/jit(_where)/select_n | solution.py:47
  30.0 55.6 %fusion.12 = bf16[12288,256]{1,0:T(8,128)(2,1)S(1)} fusion(s32[6144]{0:T(1024)S(1)} %bitcast_add_fusion, bf16[6144,128]{1,0:T(8,128)(2,1)S(1)} %iota.65, bf16[6144,128]{1,0:T(8,128)(2,1)S(1)} %select_select_fusion), kind=kOutput, calls=%fused_computation.10 | convolution fusion | flops 38739640320 | bytes 9461760 | tf_op jit(solution)/shard_map/dot_general | solution.py:57
  85.6 2.6 copy-done
  88.2 2.4 add_reduce_fusion
  90.6 7.2 %all-to-all-start = ((s32[8,1,1536]{2,1,0:T(1,128)}), s32[8,1,1536]{2,1,0:T(1,128)S(1)}, u32[]{:S(2)}, u32[]{:S(2)}) async-start(s32[8,1,1536]{2,1,0:T(1,128)} %bitcast.17), calls=%async_computation | async-start | bytes 98304 | tf_op jit(solution)/shard_map/all_to_all | solution.py:63
  97.9 3.2 slice.53
  101.1 3.6 all-to-all-done
  104.7 3.8 all-to-all-start.1
  108.8 69.2 %all-to-all-done.1 = bf16[8,1536,128]{2,1,0:T(8,128)(2,1)S(1)} async-done(((bf16[8,1536,128]{2,1,0:T(8,128)(2,1)}), bf16[8,1536,128]{2,1,0:T(8,128)(2,1)S(1)}, u32[]{:S(2)}, u32[]{:S(2)}) %all-to-all-start.1) | async-done | bytes 3145760 | tf_op jit(solution)/shard_map/all_to_all | solution.py:66
  178.0 2.8 copy.30
  180.8 5.2 %broadcast_select_fusion.2 = (bf16[12288,128]{0,1:T(8,128)(2,1)}, bf16[12288,128]{0,1:T(8,128)(2,1)}, bf16[12288,128]{0,1:T(8,128)(2,1)}) fusion(bf16[12288,128]{0,1:T(8,128)(2,1)} %copy.30, pred[12288]{0:T(1024)(128)(4,1)S(1)} %get-tuple-element.16, pred[12288]{0:T(1024)(128)(4,1)S(1)} %get-tuple-element.18, pred[12288]{0:T(1024)(128)(4,1)S(1)} %get-tuple-element.17), kind=kLoop, calls=%fused_computation.32 | loop fusion | flops 4718592 | bytes 12619776 | tf_op jit(solution)/shard_map/jit(_where)/select_n | solution.py:80
  186.0 29.8 %fusion.4 = f32[384,2304]{1,0:T(8,128)S(1)} fusion(bf16[1,1,12288,2304]{3,2,1,0:T(8,128)(2,1)} %param.9, bf16[12288,128]{0,1:T(8,128)(2,1)} %get-tuple-element.8, bf16[12288,128]{0,1:T(8,128)(2,1)} %get-tuple-element.9, bf16[12288,128]{0,1:T(8,128)(2,1)} %get-tuple-element.7), kind=kOutput, calls=%fused_computation.6 | convolution fusion | flops 21771583488 | bytes 69599232 | tf_op jit(solution)/shard_map/dot_general | solution.py:85
  215.7 2.4 reshape.162
  218.2 67.2 %reduce-scatter.2.cloned.1.call-done = f32[3,16,1152]{2,1,0:T(8,128)} async-done(((f32[3,256,1152]{2,1,0:T(8,128)}), f32[3,16,1152]{2,1,0:T(8,128)}) %reduce-scatter.2.cloned.1.call-update) | async-done | bytes 221200 | tf_op jit(solution)/shard_map/reduce_scatter | solution.py:88
  287.1 40.6 %all-gather.2.cloned.1.call-done = bf16[3,256,1152]{2,1,0:T(8,128)(2,1)} async-done(((bf16[3,16,1152]{2,1,0:T(8,128)(2,1)}), bf16[3,256,1152]{2,1,0:T(8,128)(2,1)}) %all-gather.2.cloned.1.call-update) | async-done | bytes 1769488 | tf_op jit(solution)/shard_map/all_gather | solution.py:90
  331.0 32.6 %fusion.9 = bf16[12288,384]{0,1:T(8,128)(2,1)} fusion(bf16[1,1,12288,2304]{3,2,1,0:T(8,128)(2,1)} %param.9, bf16[128,2304]{1,0:T(8,128)(2,1)S(1)} %convolution_convert_fusion, bf16[128,2304]{1,0:T(8,128)(2,1)S(1)} %convolution_convert_fusion.1, bf16[128,2304]{1,0:T(8,128)(2,1)S(1)} %convolution_convert_fusion.2), kind=kOutput, calls=%fused_computation.9 | convolution fusion | flops 21753298944 | bytes 67829760 | tf_op jit(solution)/shard_map/dot_general | solution.py:97
  363.5 4.5 fusion.19
  368.0 1.9 copy.33
  370.0 3.8 all-to-all-start.2
  375.3 69.8 %all-to-all-done.2 = bf16[8,1536,128]{1,2,0:T(8,128)(2,1)S(1)} async-done(((bf16[8,1536,128]{1,2,0:T(8,128)(2,1)}), bf16[8,1536,128]{1,2,0:T(8,128)(2,1)S(1)}, u32[]{:S(2)}, u32[]{:S(2)}) %all-to-all-start.2) | async-done | bytes 3145760 | tf_op jit(solution)/shard_map/all_to_all | solution.py:110
  445.1 3.6 copy.28
  448.7 18.9 %gather_fusion = f32[6144,128]{1,0:T(8,128)S(1)} fusion(f32[12288,128]{1,0:T(8,128)} %bitcast.49, s32[6144]{0:T(1024)S(1)} %broadcast_clamp_fusion), kind=kCustom, calls=%fused_computation | custom fusion | bytes 6316032 | tf_op jit(solution)/shard_map/gather | solution.py:113
  467.5 2.2 reshape.164
  469.7 6.6 %select_reduce_fusion.2 = (f32[1024,128]{1,0:T(8,128)S(1)}, f32[1024,128]{1,0:T(8,128)S(1)}, f32[1024,128]{1,0:T(8,128)S(1)}) fusion(f32[1024,6,128]{2,1,0:T(8,128)} %reshape.164, pred[6]{0:T(512)(128)(4,1)S(1)} %copy-done.16, pred[6]{0:T(512)(128)(4,1)S(1)} %copy-done.14, pred[6]{0:T(512)(128)(4,1)S(1)} %copy-done.18), kind=kLoop, calls=%fused_computation.19 | loop fusion | flops 4325376 | bytes 4718610 | tf_op jit(solution)/shard_map/reduce_sum | solution.py:116
  (90 shorter events, 21.4 us)
Async XLA Ops:
  7.2 6.6 %copy-start.2 = (bf16[3,1024,128]{2,1,0:T(8,128)(2,1)S(1)}, bf16[3,1024,128]{2,1,0:T(8,128)(2,1)}, u32[]{:S(2)}) copy-start(bf16[3,1024,128]{2,1,0:T(8,128)(2,1)} %param.7) | copy-start | bytes 2359300
  9.8 4.4 copy-start.11
  10.5 1.0 copy-start.15
  10.5 1.0 copy-start.17
  12.6 1.7 copy-start.1
  13.7 6.0 %copy-start.9 = (f32[48,128]{1,0:T(8,128)}, f32[48,128]{1,0:T(8,128)S(1)}, u32[]{:S(2)}) copy-start(f32[48,128]{1,0:T(8,128)S(1)} %fusion.29) | copy-start | bytes 73732
  85.6 2.7 copy-start
  90.6 14.0 %all-to-all-start = ((s32[8,1,1536]{2,1,0:T(1,128)}), s32[8,1,1536]{2,1,0:T(1,128)S(1)}, u32[]{:S(2)}, u32[]{:S(2)}) async-start(s32[8,1,1536]{2,1,0:T(1,128)} %bitcast.17), calls=%async_computation | async-start | bytes 98304 | tf_op jit(solution)/shard_map/all_to_all | solution.py:63
  104.7 3.8 copy-start.19
  104.7 73.3 %all-to-all-start.1 = ((bf16[8,1536,128]{2,1,0:T(8,128)(2,1)}), bf16[8,1536,128]{2,1,0:T(8,128)(2,1)S(1)}, u32[]{:S(2)}, u32[]{:S(2)}) async-start(bf16[8,1536,128]{2,1,0:T(8,128)(2,1)} %bitcast.7), calls=%async_computation.1 | async-start | bytes 6291456 | tf_op jit(solution)/shard_map/all_to_all | solution.py:66
  108.5 176.9 %reduce-scatter.2.cloned.1.call-start = ((), (), s32[]{:S(2)}) async-start(), calls=%async_computation.4 | async-start | bytes 3760128 | tf_op jit(solution)/shard_map/reduce_scatter | solution.py:88
  108.8 72.0 %copy-start.4 = (pred[12288]{0:T(1024)(128)(4,1)}, pred[12288]{0:T(1024)(128)(4,1)S(1)}, u32[]{:S(2)}) copy-start(pred[12288]{0:T(1024)(128)(4,1)S(1)} %get-tuple-element.17) | copy-start | bytes 36868
  108.8 72.0 %copy-start.6 = (pred[12288]{0:T(1024)(128)(4,1)}, pred[12288]{0:T(1024)(128)(4,1)S(1)}, u32[]{:S(2)}) copy-start(pred[12288]{0:T(1024)(128)(4,1)S(1)} %get-tuple-element.18) | copy-start | bytes 36868
  218.2 67.2 %copy-start.8 = (bf16[3,16,1152]{2,1,0:T(8,128)(2,1)S(1)}, bf16[3,16,1152]{2,1,0:T(8,128)(2,1)}, u32[]{:S(2)}) copy-start(bf16[3,16,1152]{2,1,0:T(8,128)(2,1)} %param.8) | copy-start | bytes 331780
  218.2 111.3 %copy-start.12 = (s32[128]{0:T(128)S(1)}, s32[128]{0:T(128)}, u32[]{:S(2)}) copy-start(s32[128]{0:T(128)} %copy-done.11) | copy-start | bytes 1540
  218.2 109.5 %all-gather.2.cloned.1.call-start = ((), (), s32[]{:S(2)}) async-start(), calls=%async_computation.5 | async-start | bytes 1880064 | tf_op jit(solution)/shard_map/all_gather | solution.py:90
  331.0 32.6 %copy-start.5 = (pred[12288]{0:T(1024)(128)(4,1)S(1)}, pred[12288]{0:T(1024)(128)(4,1)}, u32[]{:S(2)}) copy-start(pred[12288]{0:T(1024)(128)(4,1)} %copy-done.4) | copy-start | bytes 36868
  331.0 32.6 %copy-start.7 = (pred[12288]{0:T(1024)(128)(4,1)S(1)}, pred[12288]{0:T(1024)(128)(4,1)}, u32[]{:S(2)}) copy-start(pred[12288]{0:T(1024)(128)(4,1)} %copy-done.6) | copy-start | bytes 36868
  370.0 5.2 %copy-start.10 = (f32[48,128]{1,0:T(8,128)S(1)}, f32[48,128]{1,0:T(8,128)}, u32[]{:S(2)}) copy-start(f32[48,128]{1,0:T(8,128)} %copy-done.9) | copy-start | bytes 73732
  370.0 75.1 %all-to-all-start.2 = ((bf16[8,1536,128]{1,2,0:T(8,128)(2,1)}), bf16[8,1536,128]{1,2,0:T(8,128)(2,1)S(1)}, u32[]{:S(2)}, u32[]{:S(2)}) async-start(bf16[8,1536,128]{1,2,0:T(8,128)(2,1)} %bitcast.48), calls=%async_computation.3 | async-start | bytes 6291456 | tf_op jit(solution)/shard_map/all_to_all | solution.py:110
  467.5 2.2 copy-start.14
  467.5 2.2 copy-start.16
  467.5 2.2 copy-start.18
  469.7 6.6 %copy-start.3 = (bf16[3,1024,128]{2,1,0:T(8,128)(2,1)S(1)}, bf16[3,1024,128]{2,1,0:T(8,128)(2,1)}, u32[]{:S(2)}) copy-start(bf16[3,1024,128]{2,1,0:T(8,128)(2,1)} %param.7) | copy-start | bytes 2359300
  (1 other events, 1.0 us)
Sparse Core Ops, SparseCore 0:
  218.3 67.0 reduce-scatter.1
  288.3 39.3 all-gather.1

commit v2 on v1

--- a/solution.py
+++ b/solution.py
@@ -53,23 +53,35 @@
     slot_of = destination * capacity + ranks(destination, owners)
     tile_of_row = lax.broadcasted_iota(jnp.int32, (feat_dev, tile_count, tokens), 1)
     tile_of_row = (tile_of_row + 1).astype(jnp.bfloat16).reshape(count_rows, tokens)
-    slot_match = lax.broadcasted_iota(jnp.int32, (slot_count, count_rows), 0) == slot_of[None, :]
-    packed = jnp.dot(
-        slot_match.astype(jnp.bfloat16),
-        jnp.concatenate([row_values, tile_of_row], axis=1),
-        preferred_element_type=jnp.float32,
-    ).astype(jnp.bfloat16)
-    tile_slot = packed[:, tokens].astype(jnp.int32) - 1
+    payload = jnp.concatenate([row_values, tile_of_row], axis=1)
+    arrived, arrived_tiles = [], []
+    cuts = sorted({0, capacity // 2, capacity})
+    for low, high in zip(cuts[:-1], cuts[1:]):
+        span = high - low
+        owner_id = lax.broadcasted_iota(jnp.int32, (owners, span), 0)
+        offset = lax.broadcasted_iota(jnp.int32, (owners, span), 1)
+        slot_id = (owner_id * capacity + low + offset).reshape(-1)
+        slot_match = slot_id[:, None] == slot_of[None, :]
+        packed = jnp.dot(
+            slot_match.astype(jnp.bfloat16), payload, preferred_element_type=jnp.float32
+        ).astype(jnp.bfloat16)
+        arrived.append(
+            lax.all_to_all(
+                packed[:, :tokens].reshape(owners, span, tokens),
+                "tile",
+                split_axis=0,
+                concat_axis=0,
+                tiled=True,
+            )
+        )
+        arrived_tiles.append((packed[:, tokens].astype(jnp.int32) - 1).reshape(owners, span))
+    tiles, arrived[0] = lax.optimization_barrier(
+        (jnp.concatenate(arrived_tiles, axis=1), arrived[0])
+    )
     tile_recv = lax.all_to_all(
-        tile_slot.reshape(owners, capacity), "tile", split_axis=0, concat_axis=0, tiled=True
+        tiles, "tile", split_axis=0, concat_axis=0, tiled=True
     ).reshape(slot_count)
-    received = lax.all_to_all(
-        packed[:, :tokens].reshape(owners, capacity, tokens),
-        "tile",
-        split_axis=0,
-        concat_axis=0,
-        tiled=True,
-    ).reshape(slot_count, tokens)
+    received = jnp.concatenate(arrived, axis=1).reshape(slot_count, tokens)
     tile_ids = lax.broadcasted_iota(jnp.int32, (slot_count, tile_count), 1)
     target_slot = jnp.sum(
         jnp.where(tile_recv[:, None] == tile_ids, tile_target[None, :] + 1, 0), axis=1

time: 485 us -> 456 us (0.940)
  waiting for transfers between devices: 250 us -> 222 us
  matrix products: 120 us -> 109 us
    all_to_all x2 -> x3, waiting for transfers between devices: 72.7 us -> 44 us  [the longest x2 42.4 us: on_device(): lax.all_to_all(packed[:, :tokens].reshape(owners, span, tokens), 'tile',...]
    dot_general x1 -> x2, matrix products: 55.6 us -> 45.5 us  [on_device(): jnp.dot(slot_match.astype(jnp.bfloat16), payload, preferred_element_type=...]
    all_to_all x2 -> x3, starting transfers between devices: 11 us -> 14.7 us  [the longest x2 11 us: on_device(): lax.all_to_all(packed[:, :tokens].reshape(owners, span, tokens), 'tile',...]
  transfers between devices with their start and end apart: 5 -> 6, of which waited for: 5 -> 6; matrix products, arithmetic and copies ran while one was open for 1% -> 8% of each run, Pallas kernels for 0% -> 0%
where the time goes in v2:
time: 456 us; the launch traced here: 455 us
  waiting for transfers between devices  222 us (49%)
  matrix products  109 us (24%)
  local copies, waits for them, and re-layouts  52 us (11%)
  other arithmetic  37.9 us (8%)
  starting transfers between devices  19.3 us (4%)
  between operations  14.6 us (3%)
    all_to_all x1, waiting for transfers between devices, on_device(): lax.all_to_all(slot_grad.reshape(owners, capacity, tokens), 'tile', split...  69.5 us
    reduce_scatter x1, waiting for transfers between devices, on_device(): lax.psum_scatter(partial_value, ('tile', 'feat'), scatter_dimension=1, ti...  67.5 us
    dot_general x2, matrix products, on_device(): jnp.dot(slot_match.astype(jnp.bfloat16), payload, preferred_element_type=...  45.5 us
    all_to_all x2, waiting for transfers between devices, on_device(): lax.all_to_all(packed[:, :tokens].reshape(owners, span, tokens), 'tile',...  42.4 us
    all_gather x1, waiting for transfers between devices, on_device(): lax.all_gather(residual.astype(jnp.bfloat16), ('tile', 'feat'), axis=1, t...  40.5 us
    dot_general x1, matrix products, on_device(): lax.dot_general(weights, jnp.concatenate(by_column, axis=0), (((1,), (1,)...  32.4 us
    dot_general x1, matrix products, on_device(): lax.dot_general(masked, weights, (((0,), (0,)), ((), ())), preferred_elem...  29.7 us
    gather x1, local copies, waits for them, and re-layouts, on_device(): returned.astype(jnp.float32)[slot_of].reshape(feat_dev, tile_count, tokens)  18.9 us
  transfers between devices with their start and end apart: 6, of which 6 were waited for; matrix products, arithmetic and copies ran while one was open for 8% of the time, Pallas kernels for 0%

profile of v2, /device:TPU:0, one launch (start us, length us, event | category | flops | bytes accessed | tf_op | source)
XLA Modules:
  0.0 454.8 jit_solution(12843944951812199099)
XLA Ops:
  19.6 9.2 %select_select_fusion = bf16[6144,128]{1,0:T(8,128)(2,1)S(1)} fusion(bf16[6144,128]{1,0:T(8,128)(2,1)} %broadcast_in_dim.158, bf16[6144,128]{1,0:T(8,128)(2,1)} %broadcast_in_dim.164, bf16[6144,128]{1,0:T(8,128)(2,1)} %broadcast_in_dim.170, pred[6144]{0:T(1024)(128)(4,1)S(1)} %broadcast_in_dim.166, pred[6144]{0:T(1024)(128)(4,1)S(1)} %broadcast_in_dim.160, ...), kind=kLoop, calls=%fused_computation.45 | loop fusion | flops 2359296 | bytes 6309888 | tf_op jit(solution)/shard_map/jit(_where)/select_n | solution.py:47
  29.8 22.1 %fusion.23 = bf16[6144,256]{1,0:T(8,128)(2,1)S(1)} fusion(s32[6144]{0:T(1024)S(1)} %bitcast_add_fusion, s32[6144]{0:T(1024)S(1)} %add.101, bf16[6144,128]{1,0:T(8,128)(2,1)S(1)} %iota.87, bf16[6144,128]{1,0:T(8,128)(2,1)S(1)} %select_select_fusion), kind=kOutput, calls=%fused_computation.20 | convolution fusion | flops 19372965888 | bytes 6340608 | tf_op jit(solution)/shard_map/dot_general | solution.py:65
  54.8 7.3 %all-to-all-start = ((bf16[8,768,128]{2,1,0:T(8,128)(2,1)}), bf16[8,768,128]{2,1,0:T(8,128)(2,1)S(1)}, u32[]{:S(2)}, u32[]{:S(2)}) async-start(bf16[8,768,128]{2,1,0:T(8,128)(2,1)} %bitcast.6), calls=%async_computation | async-start | bytes 3145728 | tf_op jit(solution)/shard_map/all_to_all | solution.py:69
  62.2 23.4 %fusion.26 = bf16[6144,256]{1,0:T(8,128)(2,1)S(1)} fusion(s32[6144]{0:T(1024)S(1)} %bitcast_add_fusion, s32[6144]{0:T(1024)S(1)} %add.111, bf16[6144,128]{1,0:T(8,128)(2,1)S(1)} %iota.87, bf16[6144,128]{1,0:T(8,128)(2,1)} %copy-done.7), kind=kOutput, calls=%fused_computation.21 | convolution fusion | flops 19372965888 | bytes 6340608 | tf_op jit(solution)/shard_map/dot_general | solution.py:65
  88.5 10.6 %all-to-all-done = bf16[8,768,128]{2,1,0:T(8,128)(2,1)S(1)} async-done(((bf16[8,768,128]{2,1,0:T(8,128)(2,1)}), bf16[8,768,128]{2,1,0:T(8,128)(2,1)S(1)}, u32[]{:S(2)}, u32[]{:S(2)}) %all-to-all-start) | async-done | bytes 1572896 | tf_op jit(solution)/shard_map/all_to_all | solution.py:69
  99.1 3.8 all-to-all-start.2
  102.9 2.3 add_reduce_fusion.1
  105.2 2.3 add_reduce_fusion
  108.2 31.8 %all-to-all-done.2 = bf16[8,768,128]{2,1,0:T(8,128)(2,1)S(1)} async-done(((bf16[8,768,128]{2,1,0:T(8,128)(2,1)}), bf16[8,768,128]{2,1,0:T(8,128)(2,1)S(1)}, u32[]{:S(2)}, u32[]{:S(2)}) %all-to-all-start.2) | async-done | bytes 1572896 | tf_op jit(solution)/shard_map/all_to_all | solution.py:69
  140.0 3.6 all-to-all-start.1
  146.1 2.9 copy.30
  150.7 5.1 %broadcast_select_fusion.2 = (bf16[12288,128]{0,1:T(8,128)(2,1)}, bf16[12288,128]{0,1:T(8,128)(2,1)}, bf16[12288,128]{0,1:T(8,128)(2,1)}) fusion(bf16[12288,128]{0,1:T(8,128)(2,1)} %copy.30, pred[12288]{0:T(1024)(128)(4,1)S(1)} %get-tuple-element.20, pred[12288]{0:T(1024)(128)(4,1)S(1)} %get-tuple-element.22, pred[12288]{0:T(1024)(128)(4,1)S(1)} %get-tuple-element.21), kind=kLoop, calls=%fused_computation.38 | loop fusion | flops 4718592 | bytes 12619776 | tf_op jit(solution)/shard_map/jit(_where)/select_n | solution.py:92
  155.9 29.7 %fusion.10 = f32[384,2304]{1,0:T(8,128)S(1)} fusion(bf16[1,1,12288,2304]{3,2,1,0:T(8,128)(2,1)} %param.9, bf16[12288,128]{0,1:T(8,128)(2,1)} %get-tuple-element.12, bf16[12288,128]{0,1:T(8,128)(2,1)} %get-tuple-element.13, bf16[12288,128]{0,1:T(8,128)(2,1)} %get-tuple-element.11), kind=kOutput, calls=%fused_computation.11 | convolution fusion | flops 21771583488 | bytes 69599232 | tf_op jit(solution)/shard_map/dot_general | solution.py:97
  185.6 2.5 reshape.186
  188.5 67.5 %reduce-scatter.2.cloned.1.call-done = f32[3,16,1152]{2,1,0:T(8,128)} async-done(((f32[3,256,1152]{2,1,0:T(8,128)}), f32[3,16,1152]{2,1,0:T(8,128)}) %reduce-scatter.2.cloned.1.call-update) | async-done | bytes 221200 | tf_op jit(solution)/shard_map/reduce_scatter | solution.py:100
  257.7 40.5 %all-gather.2.cloned.1.call-done = bf16[3,256,1152]{2,1,0:T(8,128)(2,1)} async-done(((bf16[3,16,1152]{2,1,0:T(8,128)(2,1)}), bf16[3,256,1152]{2,1,0:T(8,128)(2,1)}) %all-gather.2.cloned.1.call-update) | async-done | bytes 1769488 | tf_op jit(solution)/shard_map/all_gather | solution.py:102
  301.5 32.4 %fusion.15 = bf16[12288,384]{0,1:T(8,128)(2,1)} fusion(bf16[1,1,12288,2304]{3,2,1,0:T(8,128)(2,1)} %param.9, bf16[128,2304]{1,0:T(8,128)(2,1)S(1)} %convolution_convert_fusion, bf16[128,2304]{1,0:T(8,128)(2,1)S(1)} %convolution_convert_fusion.1, bf16[128,2304]{1,0:T(8,128)(2,1)S(1)} %convolution_convert_fusion.2), kind=kOutput, calls=%fused_computation.14 | convolution fusion | flops 21753298944 | bytes 67829760 | tf_op jit(solution)/shard_map/dot_general | solution.py:109
  333.9 4.5 fusion.30
  340.3 4.1 all-to-all-start.3
  345.9 69.5 %all-to-all-done.3 = bf16[8,1536,128]{1,2,0:T(8,128)(2,1)S(1)} async-done(((bf16[8,1536,128]{1,2,0:T(8,128)(2,1)}), bf16[8,1536,128]{1,2,0:T(8,128)(2,1)S(1)}, u32[]{:S(2)}, u32[]{:S(2)}) %all-to-all-start.3) | async-done | bytes 3145760 | tf_op jit(solution)/shard_map/all_to_all | solution.py:122
  415.4 3.6 copy.28
  419.0 18.9 %gather_fusion = f32[6144,128]{1,0:T(8,128)S(1)} fusion(f32[12288,128]{1,0:T(8,128)} %bitcast.50, s32[6144]{0:T(1024)S(1)} %broadcast_clamp_fusion), kind=kCustom, calls=%fused_computation | custom fusion | bytes 6316032 | tf_op jit(solution)/shard_map/gather | solution.py:125
  437.9 2.2 reshape.188
  440.1 6.6 %select_reduce_fusion.2 = (f32[1024,128]{1,0:T(8,128)S(1)}, f32[1024,128]{1,0:T(8,128)S(1)}, f32[1024,128]{1,0:T(8,128)S(1)}) fusion(f32[1024,6,128]{2,1,0:T(8,128)} %reshape.188, pred[6]{0:T(512)(128)(4,1)S(1)} %copy-done.20, pred[6]{0:T(512)(128)(4,1)S(1)} %copy-done.18, pred[6]{0:T(512)(128)(4,1)S(1)} %copy-done.22), kind=kLoop, calls=%fused_computation.24 | loop fusion | flops 4325376 | bytes 4718610 | tf_op jit(solution)/shard_map/reduce_sum | solution.py:128
  (114 shorter events, 33.9 us)
Async XLA Ops:
  7.2 6.7 %copy-start.5 = (bf16[3,1024,128]{2,1,0:T(8,128)(2,1)S(1)}, bf16[3,1024,128]{2,1,0:T(8,128)(2,1)}, u32[]{:S(2)}) copy-start(bf16[3,1024,128]{2,1,0:T(8,128)(2,1)} %param.7) | copy-start | bytes 2359300
  9.8 4.5 copy-start.15
  13.8 5.8 %copy-start.13 = (f32[48,128]{1,0:T(8,128)}, f32[48,128]{1,0:T(8,128)S(1)}, u32[]{:S(2)}) copy-start(f32[48,128]{1,0:T(8,128)S(1)} %fusion.37) | copy-start | bytes 73732
  28.8 23.1 %copy-start.7 = (bf16[6144,128]{1,0:T(8,128)(2,1)}, bf16[6144,128]{1,0:T(8,128)(2,1)S(1)}, u32[]{:S(2)}) copy-start(bf16[6144,128]{1,0:T(8,128)(2,1)S(1)} %select_select_fusion) | copy-start | bytes 4718596
  54.8 44.3 %all-to-all-start = ((bf16[8,768,128]{2,1,0:T(8,128)(2,1)}), bf16[8,768,128]{2,1,0:T(8,128)(2,1)S(1)}, u32[]{:S(2)}, u32[]{:S(2)}) async-start(bf16[8,768,128]{2,1,0:T(8,128)(2,1)} %bitcast.6), calls=%async_computation | async-start | bytes 3145728 | tf_op jit(solution)/shard_map/all_to_all | solution.py:69
  99.1 8.4 %copy-start = (bf16[8,768,128]{2,1,0:T(8,128)(2,1)}, bf16[8,768,128]{2,1,0:T(8,128)(2,1)S(1)}, u32[]{:S(2)}) copy-start(bf16[8,768,128]{2,1,0:T(8,128)(2,1)S(1)} %all-to-all-done) | copy-start | bytes 4718596
  99.1 8.4 %copy-start.23 = (s32[6]{0:T(128)S(1)}, s32[6]{0:T(128)}, u32[]{:S(2)}) copy-start(s32[6]{0:T(128)} %param.12) | copy-start | bytes 76
  99.1 41.0 %all-to-all-start.2 = ((bf16[8,768,128]{2,1,0:T(8,128)(2,1)}), bf16[8,768,128]{2,1,0:T(8,128)(2,1)S(1)}, u32[]{:S(2)}, u32[]{:S(2)}) async-start(bf16[8,768,128]{2,1,0:T(8,128)(2,1)} %bitcast.9), calls=%async_computation.2 | async-start | bytes 3145728 | tf_op jit(solution)/shard_map/all_to_all | solution.py:69
  140.0 3.6 copy-start.1
  140.0 10.4 %all-to-all-start.1 = ((s32[8,1,1536]{2,1,0:T(1,128)}), s32[8,1,1536]{2,1,0:T(1,128)S(1)}, u32[]{:S(2)}, u32[]{:S(2)}) async-start(s32[8,1,1536]{2,1,0:T(1,128)} %copy.25), calls=%async_computation.1 | async-start | bytes 98304 | tf_op jit(solution)/shard_map/all_to_all | solution.py:81
  143.7 112.3 %reduce-scatter.2.cloned.1.call-start = ((), (), s32[]{:S(2)}) async-start(), calls=%async_computation.5 | async-start | bytes 3760128 | tf_op jit(solution)/shard_map/reduce_scatter | solution.py:100
  150.7 5.2 %copy-start.8 = (pred[12288]{0:T(1024)(128)(4,1)}, pred[12288]{0:T(1024)(128)(4,1)S(1)}, u32[]{:S(2)}) copy-start(pred[12288]{0:T(1024)(128)(4,1)S(1)} %get-tuple-element.21) | copy-start | bytes 36868
  150.7 5.2 %copy-start.10 = (pred[12288]{0:T(1024)(128)(4,1)}, pred[12288]{0:T(1024)(128)(4,1)S(1)}, u32[]{:S(2)}) copy-start(pred[12288]{0:T(1024)(128)(4,1)S(1)} %get-tuple-element.22) | copy-start | bytes 36868
  188.1 67.9 %copy-start.12 = (bf16[3,16,1152]{2,1,0:T(8,128)(2,1)S(1)}, bf16[3,16,1152]{2,1,0:T(8,128)(2,1)}, u32[]{:S(2)}) copy-start(bf16[3,16,1152]{2,1,0:T(8,128)(2,1)} %param.8) | copy-start | bytes 331780
  188.2 111.8 %copy-start.16 = (s32[128]{0:T(128)S(1)}, s32[128]{0:T(128)}, u32[]{:S(2)}) copy-start(s32[128]{0:T(128)} %copy-done.15) | copy-start | bytes 1540
  188.2 110.0 %all-gather.2.cloned.1.call-start = ((), (), s32[]{:S(2)}) async-start(), calls=%async_computation.6 | async-start | bytes 1880064 | tf_op jit(solution)/shard_map/all_gather | solution.py:102
  301.5 32.4 %copy-start.9 = (pred[12288]{0:T(1024)(128)(4,1)S(1)}, pred[12288]{0:T(1024)(128)(4,1)}, u32[]{:S(2)}) copy-start(pred[12288]{0:T(1024)(128)(4,1)} %copy-done.8) | copy-start | bytes 36868
  301.5 32.4 %copy-start.11 = (pred[12288]{0:T(1024)(128)(4,1)S(1)}, pred[12288]{0:T(1024)(128)(4,1)}, u32[]{:S(2)}) copy-start(pred[12288]{0:T(1024)(128)(4,1)} %copy-done.10) | copy-start | bytes 36868
  340.3 5.5 %copy-start.14 = (f32[48,128]{1,0:T(8,128)S(1)}, f32[48,128]{1,0:T(8,128)}, u32[]{:S(2)}) copy-start(f32[48,128]{1,0:T(8,128)} %copy-done.13) | copy-start | bytes 73732
  340.3 75.1 %all-to-all-start.3 = ((bf16[8,1536,128]{1,2,0:T(8,128)(2,1)}), bf16[8,1536,128]{1,2,0:T(8,128)(2,1)S(1)}, u32[]{:S(2)}, u32[]{:S(2)}) async-start(bf16[8,1536,128]{1,2,0:T(8,128)(2,1)} %bitcast.49), calls=%async_computation.4 | async-start | bytes 6291456 | tf_op jit(solution)/shard_map/all_to_all | solution.py:122
  437.9 2.2 copy-start.18
  437.9 2.2 copy-start.20
  437.9 2.2 copy-start.22
  440.1 6.6 %copy-start.6 = (bf16[3,1024,128]{2,1,0:T(8,128)(2,1)S(1)}, bf16[3,1024,128]{2,1,0:T(8,128)(2,1)}, u32[]{:S(2)}) copy-start(bf16[3,1024,128]{2,1,0:T(8,128)(2,1)} %param.7) | copy-start | bytes 2359300
  (6 other events, 7.7 us)
Sparse Core Ops, SparseCore 0:
  188.3 67.6 reduce-scatter.1
  258.9 39.2 all-gather.1

commit v3 on v2

--- a/solution.py
+++ b/solution.py
@@ -106,22 +106,28 @@
         jnp.dot(to_token, spread[layer], preferred_element_type=jnp.float32).astype(jnp.bfloat16)
         for layer in range(layers)
     ]
-    product = lax.dot_general(
-        weights,
-        jnp.concatenate(by_column, axis=0),
-        (((1,), (1,)), ((), ())),
-        preferred_element_type=jnp.float32,
-    ).astype(jnp.bfloat16)
-    slot_grad = jnp.zeros((slot_count, tokens), jnp.bfloat16)
-    for layer in range(layers):
-        slot_grad = jnp.where(
-            (target_slot == layer)[:, None],
-            product[:, layer * tokens : (layer + 1) * tokens],
-            slot_grad,
+    columns = jnp.concatenate(by_column, axis=0)
+    shaped = weights.reshape(owners, capacity, model_width)
+    target_of = target_slot.reshape(owners, capacity)
+    pieces = []
+    for low, high in zip(cuts[:-1], cuts[1:]):
+        product = lax.dot_general(
+            shaped[:, low:high],
+            columns,
+            (((2,), (1,)), ((), ())),
+            preferred_element_type=jnp.float32,
+        ).astype(jnp.bfloat16)
+        slot_grad = jnp.zeros((owners, high - low, tokens), jnp.bfloat16)
+        for layer in range(layers):
+            slot_grad = jnp.where(
+                (target_of[:, low:high] == layer)[:, :, None],
+                product[:, :, layer * tokens : (layer + 1) * tokens],
+                slot_grad,
+            )
+        pieces.append(
+            lax.all_to_all(slot_grad, "tile", split_axis=0, concat_axis=0, tiled=True)
         )
-    returned = lax.all_to_all(
-        slot_grad.reshape(owners, capacity, tokens), "tile", split_axis=0, concat_axis=0, tiled=True
-    ).reshape(slot_count, tokens)
+    returned = jnp.concatenate(pieces, axis=1).reshape(slot_count, tokens)
     row_grad = returned.astype(jnp.float32)[slot_of].reshape(feat_dev, tile_count, tokens)
     layer_grad = jnp.stack(
         [

time: 456 us -> 460 us (level); the launches traced: 455 us -> 452 us
  waiting for transfers between devices: 222 us -> 205 us
  other arithmetic: 37.9 us -> 48.7 us
    all_to_all x1 -> x2, waiting for transfers between devices: 69.5 us -> 52.6 us  [on_device(): lax.all_to_all(slot_grad, 'tile', split_axis=0, concat_axis=0, tiled=True)]
    select_n x1, other arithmetic: 5.15 us -> 11 us  [on_device(): jnp.where((target_slot == layer)[:, None], received, jnp.zeros_like(recei...]
    reshape x2 -> x0, local copies, waits for them, and re-layouts: 4.8 us -> none  [the longest x1 2.86 us: on_device(): received = jnp.concatenate(arrived, axis=1).reshape(slot_count, tokens)]
    dot_general x1 -> x2, matrix products: 32.4 us -> 32.2 us  [on_device(): lax.dot_general(shaped[:, low:high], columns, (((2,), (1,)), ((), ())), p...]
  transfers between devices with their start and end apart: 6 -> 7, of which waited for: 6 -> 7; matrix products, arithmetic and copies ran while one was open for 8% -> 12% of each run, Pallas kernels for 0% -> 0%
where the time goes in v3:
time: 460 us; the launch traced here: 452 us
  waiting for transfers between devices  205 us (45%)
  matrix products  110 us (24%)
  local copies, waits for them, and re-layouts  50.8 us (11%)
  other arithmetic  48.7 us (11%)
  starting transfers between devices  23.2 us (5%)
  between operations  14.9 us (3%)
    reduce_scatter x1, waiting for transfers between devices, on_device(): lax.psum_scatter(partial_value, ('tile', 'feat'), scatter_dimension=1, ti...  65.4 us
    all_to_all x2, waiting for transfers between devices, on_device(): lax.all_to_all(slot_grad, 'tile', split_axis=0, concat_axis=0, tiled=True)  52.6 us
    dot_general x2, matrix products, on_device(): jnp.dot(slot_match.astype(jnp.bfloat16), payload, preferred_element_type=...  45.5 us
    all_to_all x2, waiting for transfers between devices, on_device(): lax.all_to_all(packed[:, :tokens].reshape(owners, span, tokens), 'tile',...  42.4 us
    all_gather x1, waiting for transfers between devices, on_device(): lax.all_gather(residual.astype(jnp.bfloat16), ('tile', 'feat'), axis=1, t...  39.8 us
    dot_general x2, matrix products, on_device(): lax.dot_general(shaped[:, low:high], columns, (((2,), (1,)), ((), ())), p...  32.2 us
    dot_general x1, matrix products, on_device(): lax.dot_general(masked, weights, (((0,), (0,)), ((), ())), preferred_elem...  30.2 us
    gather x1, local copies, waits for them, and re-layouts, on_device(): returned.astype(jnp.float32)[slot_of].reshape(feat_dev, tile_count, tokens)  18.9 us
  transfers between devices with their start and end apart: 7, of which 7 were waited for; matrix products, arithmetic and copies ran while one was open for 12% of the time, Pallas kernels for 0%

profile of v3, /device:TPU:0, one launch (start us, length us, event | category | flops | bytes accessed | tf_op | source)
XLA Modules:
  0.0 452.5 jit_solution(13211649401233162780)
XLA Ops:
  19.6 9.2 %select_select_fusion = bf16[6144,128]{1,0:T(8,128)(2,1)S(1)} fusion(bf16[6144,128]{1,0:T(8,128)(2,1)} %broadcast_in_dim.185, bf16[6144,128]{1,0:T(8,128)(2,1)} %broadcast_in_dim.191, bf16[6144,128]{1,0:T(8,128)(2,1)} %broadcast_in_dim.197, pred[6144]{0:T(1024)(128)(4,1)S(1)} %broadcast_in_dim.193, pred[6144]{0:T(1024)(128)(4,1)S(1)} %broadcast_in_dim.187, ...), kind=kLoop, calls=%fused_computation.46 | loop fusion | flops 2359296 | bytes 6309888 | tf_op jit(solution)/shard_map/jit(_where)/select_n | solution.py:47
  29.9 22.1 %fusion.19 = bf16[6144,256]{1,0:T(8,128)(2,1)S(1)} fusion(s32[6144]{0:T(1024)S(1)} %bitcast_add_fusion, s32[6144]{0:T(1024)S(1)} %add.103, bf16[6144,128]{1,0:T(8,128)(2,1)S(1)} %iota.87, bf16[6144,128]{1,0:T(8,128)(2,1)S(1)} %select_select_fusion), kind=kOutput, calls=%fused_computation.20 | convolution fusion | flops 19372965888 | bytes 6340608 | tf_op jit(solution)/shard_map/dot_general | solution.py:65
  54.8 7.8 %all-to-all-start = ((bf16[8,768,128]{2,1,0:T(8,128)(2,1)}), bf16[8,768,128]{2,1,0:T(8,128)(2,1)S(1)}, u32[]{:S(2)}, u32[]{:S(2)}) async-start(bf16[8,768,128]{2,1,0:T(8,128)(2,1)} %bitcast.6), calls=%async_computation | async-start | bytes 3145728 | tf_op jit(solution)/shard_map/all_to_all | solution.py:69
  62.7 23.4 %fusion.22 = bf16[6144,256]{1,0:T(8,128)(2,1)S(1)} fusion(s32[6144]{0:T(1024)S(1)} %bitcast_add_fusion, s32[6144]{0:T(1024)S(1)} %add.113, bf16[6144,128]{1,0:T(8,128)(2,1)S(1)} %iota.87, bf16[6144,128]{1,0:T(8,128)(2,1)} %copy-done.7), kind=kOutput, calls=%fused_computation.21 | convolution fusion | flops 19372965888 | bytes 6340608 | tf_op jit(solution)/shard_map/dot_general | solution.py:65
  89.1 10.5 %all-to-all-done = bf16[8,768,128]{2,1,0:T(8,128)(2,1)S(1)} async-done(((bf16[8,768,128]{2,1,0:T(8,128)(2,1)}), bf16[8,768,128]{2,1,0:T(8,128)(2,1)S(1)}, u32[]{:S(2)}, u32[]{:S(2)}) %all-to-all-start) | async-done | bytes 1572896 | tf_op jit(solution)/shard_map/all_to_all | solution.py:69
  99.6 3.8 all-to-all-start.2
  108.7 31.8 %all-to-all-done.2 = bf16[8,768,128]{2,1,0:T(8,128)(2,1)S(1)} async-done(((bf16[8,768,128]{2,1,0:T(8,128)(2,1)}), bf16[8,768,128]{2,1,0:T(8,128)(2,1)S(1)}, u32[]{:S(2)}, u32[]{:S(2)}) %all-to-all-start.2) | async-done | bytes 1572896 | tf_op jit(solution)/shard_map/all_to_all | solution.py:69
  140.6 3.6 all-to-all-start.1
  146.5 4.5 all-to-all-done.1
  151.8 11.0 %bitcast_select_fusion.2 = (bf16[12288,128]{1,0:T(8,128)(2,1)}, bf16[12288,128]{1,0:T(8,128)(2,1)}, bf16[12288,128]{1,0:T(8,128)(2,1)}) fusion(bf16[8,1536,128]{2,1,0:T(8,128)(2,1)S(1)} %pad_maximum_fusion.1, pred[12288]{0:T(1024)(128)(4,1)S(1)} %get-tuple-element.26, pred[12288]{0:T(1024)(128)(4,1)S(1)} %get-tuple-element.27, ...), kind=kLoop, calls=%fused_computation.35 | loop fusion | flops 4718592 | bytes 12619776 | tf_op jit(solution)/shard_map/jit(_where)/select_n | solution.py:92
  162.9 30.2 %fusion.8 = f32[384,2304]{1,0:T(8,128)S(1)} fusion(bf16[1,1,12288,2304]{3,2,1,0:T(8,128)(2,1)} %param.9, bf16[12288,128]{1,0:T(8,128)(2,1)} %get-tuple-element.13, bf16[12288,128]{1,0:T(8,128)(2,1)} %get-tuple-element.12, bf16[12288,128]{1,0:T(8,128)(2,1)} %get-tuple-element.11), kind=kOutput, calls=%fused_computation.9 | convolution fusion | flops 21771583488 | bytes 69599232 | tf_op jit(solution)/shard_map/dot_general | solution.py:97
  195.8 65.4 %reduce-scatter.2.cloned.1.call-done = f32[3,16,1152]{2,1,0:T(8,128)} async-done(((f32[3,256,1152]{2,1,0:T(8,128)}), f32[3,16,1152]{2,1,0:T(8,128)}) %reduce-scatter.2.cloned.1.call-update) | async-done | bytes 221200 | tf_op jit(solution)/shard_map/reduce_scatter | solution.py:100
  263.6 39.8 %all-gather.2.cloned.1.call-done = bf16[3,256,1152]{2,1,0:T(8,128)(2,1)} async-done(((bf16[3,16,1152]{2,1,0:T(8,128)(2,1)}), bf16[3,256,1152]{2,1,0:T(8,128)(2,1)}) %all-gather.2.cloned.1.call-update) | async-done | bytes 1769488 | tf_op jit(solution)/shard_map/all_gather | solution.py:102
  307.3 15.4 %convert_bitcast_fusion = bf16[8,768,384]{1,2,0:T(8,128)(2,1)S(1)} fusion(bf16[8,1536,2304]{2,1,0:T(8,128)(2,1)} %bitcast.58, bf16[128,2304]{1,0:T(8,128)(2,1)S(1)} %convolution_convert_fusion, bf16[128,2304]{1,0:T(8,128)(2,1)S(1)} %convolution_convert_fusion.1, bf16[128,2304]{1,0:T(8,128)(2,1)S(1)} %convolution_convert_fusion.2), kind=kOutput, calls=%fused_computation.22 | convolution fusion | flops 10879303680 | bytes 34799616 | tf_op jit(solution)/shard_map/dot_general | solution.py:114
  324.1 3.6 all-to-all-start.4
  327.7 16.9 %convert_bitcast_fusion.1 = bf16[8,768,384]{1,2,0:T(8,128)(2,1)} fusion(bf16[8,1536,2304]{2,1,0:T(8,128)(2,1)} %bitcast.59, bf16[128,2304]{1,0:T(8,128)(2,1)S(1)} %convolution_convert_fusion, bf16[128,2304]{1,0:T(8,128)(2,1)S(1)} %convolution_convert_fusion.1, bf16[128,2304]{1,0:T(8,128)(2,1)S(1)} %convolution_convert_fusion.2), kind=kOutput, calls=%fused_computation.23 | convolution fusion | flops 10879303680 | bytes 34799616 | tf_op jit(solution)/shard_map/dot_general | solution.py:114
  344.6 3.8 fusion.32
  348.4 16.9 %all-to-all-done.4 = bf16[8,768,128]{1,2,0:T(8,128)(2,1)S(1)} async-done(((bf16[8,768,128]{1,2,0:T(8,128)(2,1)}), bf16[8,768,128]{1,2,0:T(8,128)(2,1)S(1)}, u32[]{:S(2)}, u32[]{:S(2)}) %all-to-all-start.4) | async-done | bytes 1572896 | tf_op jit(solution)/shard_map/all_to_all | solution.py:128
  365.3 3.9 all-to-all-start.3
  370.7 35.7 %all-to-all-done.3 = bf16[8,768,128]{1,2,0:T(8,128)(2,1)S(1)} async-done(((bf16[8,768,128]{1,2,0:T(8,128)(2,1)}), bf16[8,768,128]{1,2,0:T(8,128)(2,1)S(1)}, u32[]{:S(2)}, u32[]{:S(2)}) %all-to-all-start.3) | async-done | bytes 1572896 | tf_op jit(solution)/shard_map/all_to_all | solution.py:128
  406.4 3.5 maximum_convert_fusion
  409.9 6.6 %copy.21 = f32[8,1536,128]{2,1,0:T(8,128)} copy(f32[8,1536,128]{1,2,0:T(8,128)} %maximum_convert_fusion) | data formatting | bytes 12582912 | tf_op jit(solution)/shard_map/convert_element_type | solution.py:131
  416.4 18.9 %gather_fusion = f32[6144,128]{1,0:T(8,128)S(1)} fusion(f32[12288,128]{1,0:T(8,128)} %bitcast.50, s32[6144]{0:T(1024)S(1)} %broadcast_clamp_fusion), kind=kCustom, calls=%fused_computation | custom fusion | bytes 6316032 | tf_op jit(solution)/shard_map/gather | solution.py:131
  437.5 6.6 %select_reduce_fusion.2 = (f32[1024,128]{1,0:T(8,128)S(1)}, f32[1024,128]{1,0:T(8,128)S(1)}, f32[1024,128]{1,0:T(8,128)S(1)}) fusion(f32[1024,6,128]{2,1,0:T(8,128)} %reshape.194, pred[6]{0:T(512)(128)(4,1)S(1)} %copy-done.22, pred[6]{0:T(512)(128)(4,1)S(1)} %copy-done.20, pred[6]{0:T(512)(128)(4,1)S(1)} %copy-done.24), kind=kLoop, calls=%fused_computation.26 | loop fusion | flops 4325376 | bytes 4718610 | tf_op jit(solution)/shard_map/reduce_sum | solution.py:134
  (124 shorter events, 42.8 us)
Async XLA Ops:
  7.2 6.7 %copy-start.5 = (bf16[3,1024,128]{2,1,0:T(8,128)(2,1)S(1)}, bf16[3,1024,128]{2,1,0:T(8,128)(2,1)}, u32[]{:S(2)}) copy-start(bf16[3,1024,128]{2,1,0:T(8,128)(2,1)} %param.7) | copy-start | bytes 2359300
  9.8 4.5 copy-start.17
  13.8 5.8 %copy-start.11 = (f32[48,128]{1,0:T(8,128)}, f32[48,128]{1,0:T(8,128)S(1)}, u32[]{:S(2)}) copy-start(f32[48,128]{1,0:T(8,128)S(1)} %fusion.34) | copy-start | bytes 73732
  28.9 23.1 %copy-start.7 = (bf16[6144,128]{1,0:T(8,128)(2,1)}, bf16[6144,128]{1,0:T(8,128)(2,1)S(1)}, u32[]{:S(2)}) copy-start(bf16[6144,128]{1,0:T(8,128)(2,1)S(1)} %select_select_fusion) | copy-start | bytes 4718596
  54.8 44.8 %all-to-all-start = ((bf16[8,768,128]{2,1,0:T(8,128)(2,1)}), bf16[8,768,128]{2,1,0:T(8,128)(2,1)S(1)}, u32[]{:S(2)}, u32[]{:S(2)}) async-start(bf16[8,768,128]{2,1,0:T(8,128)(2,1)} %bitcast.6), calls=%async_computation | async-start | bytes 3145728 | tf_op jit(solution)/shard_map/all_to_all | solution.py:69
  99.6 8.4 %copy-start = (bf16[8,768,128]{2,1,0:T(8,128)(2,1)}, bf16[8,768,128]{2,1,0:T(8,128)(2,1)S(1)}, u32[]{:S(2)}) copy-start(bf16[8,768,128]{2,1,0:T(8,128)(2,1)S(1)} %all-to-all-done) | copy-start | bytes 4718596
  99.6 8.4 %copy-start.25 = (s32[6]{0:T(128)S(1)}, s32[6]{0:T(128)}, u32[]{:S(2)}) copy-start(s32[6]{0:T(128)} %param.12) | copy-start | bytes 76
  99.6 41.0 %all-to-all-start.2 = ((bf16[8,768,128]{2,1,0:T(8,128)(2,1)}), bf16[8,768,128]{2,1,0:T(8,128)(2,1)S(1)}, u32[]{:S(2)}, u32[]{:S(2)}) async-start(bf16[8,768,128]{2,1,0:T(8,128)(2,1)} %bitcast.9), calls=%async_computation.2 | async-start | bytes 3145728 | tf_op jit(solution)/shard_map/all_to_all | solution.py:69
  140.6 3.6 copy-start.1
  140.6 10.4 %all-to-all-start.1 = ((s32[8,1,1536]{2,1,0:T(1,128)}), s32[8,1,1536]{2,1,0:T(1,128)S(1)}, u32[]{:S(2)}, u32[]{:S(2)}) async-start(s32[8,1,1536]{2,1,0:T(1,128)} %copy.20), calls=%async_computation.1 | async-start | bytes 98304 | tf_op jit(solution)/shard_map/all_to_all | solution.py:81
  144.2 117.0 %reduce-scatter.2.cloned.1.call-start = ((), (), s32[]{:S(2)}) async-start(), calls=%async_computation.6 | async-start | bytes 3760128 | tf_op jit(solution)/shard_map/reduce_scatter | solution.py:100
  195.5 65.7 %copy-start.10 = (bf16[3,16,1152]{2,1,0:T(8,128)(2,1)S(1)}, bf16[3,16,1152]{2,1,0:T(8,128)(2,1)}, u32[]{:S(2)}) copy-start(bf16[3,16,1152]{2,1,0:T(8,128)(2,1)} %param.8) | copy-start | bytes 331780
  195.5 67.4 %copy-start.9 = (s32[12288]{0:T(1024)S(1)}, s32[12288]{0:T(1024)}, u32[]{:S(2)}) copy-start(s32[12288]{0:T(1024)} %copy-done.8) | copy-start | bytes 147460
  195.5 109.7 %copy-start.18 = (s32[128]{0:T(128)S(1)}, s32[128]{0:T(128)}, u32[]{:S(2)}) copy-start(s32[128]{0:T(128)} %copy-done.17) | copy-start | bytes 1540
  195.5 107.9 %all-gather.2.cloned.1.call-start = ((), (), s32[]{:S(2)}) async-start(), calls=%async_computation.7 | async-start | bytes 1880064 | tf_op jit(solution)/shard_map/all_gather | solution.py:102
  307.3 15.4 %copy-start.14 = (pred[8,768]{1,0:T(8,128)(4,1)S(1)}, pred[8,768]{1,0:T(8,128)(4,1)}, u32[]{:S(2)}) copy-start(pred[8,768]{1,0:T(8,128)(4,1)} %get-tuple-element.23) | copy-start | bytes 18436
  307.3 15.4 %copy-start.15 = (pred[8,768]{1,0:T(8,128)(4,1)S(1)}, pred[8,768]{1,0:T(8,128)(4,1)}, u32[]{:S(2)}) copy-start(pred[8,768]{1,0:T(8,128)(4,1)} %get-tuple-element.24) | copy-start | bytes 18436
  307.3 15.4 %copy-start.16 = (pred[8,768]{1,0:T(8,128)(4,1)S(1)}, pred[8,768]{1,0:T(8,128)(4,1)}, u32[]{:S(2)}) copy-start(pred[8,768]{1,0:T(8,128)(4,1)} %get-tuple-element.25) | copy-start | bytes 18436
  324.1 41.2 %all-to-all-start.4 = ((bf16[8,768,128]{1,2,0:T(8,128)(2,1)}), bf16[8,768,128]{1,2,0:T(8,128)(2,1)S(1)}, u32[]{:S(2)}, u32[]{:S(2)}) async-start(bf16[8,768,128]{1,2,0:T(8,128)(2,1)} %fusion.30), calls=%async_computation.5 | async-start | bytes 3145728 | tf_op jit(solution)/shard_map/all_to_all | solution.py:128
  327.7 16.9 %copy-start.13 = (pred[8,768]{1,0:T(8,128)(4,1)S(1)}, pred[8,768]{1,0:T(8,128)(4,1)}, u32[]{:S(2)}) copy-start(pred[8,768]{1,0:T(8,128)(4,1)} %get-tuple-element.22) | copy-start | bytes 18436
  348.4 22.2 %copy-start.12 = (f32[48,128]{1,0:T(8,128)S(1)}, f32[48,128]{1,0:T(8,128)}, u32[]{:S(2)}) copy-start(f32[48,128]{1,0:T(8,128)} %copy-done.11) | copy-start | bytes 73732
  365.3 41.1 %all-to-all-start.3 = ((bf16[8,768,128]{1,2,0:T(8,128)(2,1)}), bf16[8,768,128]{1,2,0:T(8,128)(2,1)S(1)}, u32[]{:S(2)}, u32[]{:S(2)}) async-start(bf16[8,768,128]{1,2,0:T(8,128)(2,1)} %fusion.32), calls=%async_computation.4 | async-start | bytes 3145728 | tf_op jit(solution)/shard_map/all_to_all | solution.py:128
  435.3 2.2 copy-start.20
  437.5 6.6 %copy-start.6 = (bf16[3,1024,128]{2,1,0:T(8,128)(2,1)S(1)}, bf16[3,1024,128]{2,1,0:T(8,128)(2,1)}, u32[]{:S(2)}) copy-start(bf16[3,1024,128]{2,1,0:T(8,128)(2,1)} %param.7) | copy-start | bytes 2359300
  (9 other events, 12.6 us)
Sparse Core Ops, SparseCore 0:
  195.6 65.5 reduce-scatter.1
  264.1 39.2 all-gather.1
